TPU v7x, 32 devices: a whole 2x2x4 slice. The times are simulated.
32 devices in a mesh: group: 2 (over x), patch: 8 (over z, y), tensor: 2 (over core).
Axes of the slice: x: 2, y: 2, z: 4, core: 2. Of those that a mesh axis runs over, the one named last changes fastest.
Arguments:
- hidden: bfloat16 [2, 1152, 3072], P(None, ('group', 'patch')), parts along dimension 1, may hold values from -6 to 6
- w_q: bfloat16 [3072, 1536], P(None, 'tensor'), may hold values from -0.109375 to 0.109375
- fresh_kv: bfloat16 [2, 1152, 2, 1536], P(None, ('group', 'patch'), None, 'tensor'), parts along dimension 1, may hold values from -6 to 6
- prev_kv: bfloat16 [1152, 2, 1536], P(('group', 'patch'), None, 'tensor'), parts along dimension 0, may hold values from -6 to 6
- exps: int32 [1152, 2, 12], P(('group', 'patch'), None, 'tensor'), parts along dimension 0, may hold values from 0 to 2
- w_out: bfloat16 [1536, 3072], P('tensor'), may hold values from -0.15625 to 0.15625
Outputs:
- mixed: bfloat16 [2, 1152, 3072], P(None, ('group', 'patch'), 'tensor'), parts along dimension 1
There are 2 independent parts, one for each index of `group`. A program takes and returns all parts, laid end to end along the dimension named above; an argument that names none is the same for every part. Nothing has to cross between parts.
All inputs are finite; a program needn't handle non-finite values.
Results may differ from a plain program's by a relative error of at most 0.008.
Values may be sent and summed in bfloat16 or wider, within the bound.
A program may use at most 128 MiB of HBM per device.

v0:
```python
import jax
import jax.numpy as jnp
from jax import lax
from jax.sharding import PartitionSpec as P

HD = 128
STEPS = 2


clip_limit = 1.0


def attend(queries, key_table, head_count):
    head_size = queries.shape[1] // head_count
    key_rows = key_table.shape[0]
    query_heads = queries.reshape(queries.shape[0], head_count, head_size)
    key_heads = key_table[:, 0].reshape(key_rows, head_count, head_size)
    value_heads = key_table[:, 1].reshape(key_rows, head_count, head_size)
    scores = jnp.einsum(
        "qhd,khd->hqk", query_heads, key_heads, preferred_element_type=jnp.float32
    ) * head_size ** (-0.5)
    weights = jax.nn.softmax(scores, axis=-1).astype(jnp.bfloat16)
    result = jnp.einsum("hqk,khd->qhd", weights, value_heads, preferred_element_type=jnp.float32)
    return result.astype(jnp.bfloat16).reshape(queries.shape)


def on_device(hidden, w_q, fresh_kv, prev_kv, exps, w_out):
    tok_rows = hidden.shape[1]
    head_count = exps.shape[2]
    query = jnp.einsum("std,de->ste", hidden, w_q, preferred_element_type=jnp.float32).astype(
        jnp.bfloat16
    )
    factor = jnp.repeat(jnp.exp2(-exps.astype(jnp.float32)), HD, axis=2)
    scaled = jnp.clip(
        (fresh_kv[0].astype(jnp.float32) - prev_kv.astype(jnp.float32)) * factor,
        -clip_limit,
        clip_limit,
    ).astype(jnp.bfloat16)
    update = (scaled.astype(jnp.float32) / factor).astype(jnp.bfloat16)
    previous_all = lax.all_gather(prev_kv, "patch", axis=0, tiled=True)
    update_all = lax.all_gather(update, "patch", axis=0, tiled=True)
    copy_all = (previous_all.astype(jnp.float32) + update_all.astype(jnp.float32)).astype(
        jnp.bfloat16
    )
    own_start = lax.axis_index("patch") * tok_rows
    results = []
    for step, stale_keys in ((0, previous_all), (1, copy_all)):
        key_table = lax.dynamic_update_slice_in_dim(stale_keys, fresh_kv[step], own_start, 0)
        results.append(attend(query[step], key_table, head_count))
    attended = jnp.stack(results)
    flat_rows = attended.reshape(STEPS * tok_rows, attended.shape[2])
    partial_value = jnp.dot(flat_rows, w_out, preferred_element_type=jnp.float32)
    summed = lax.psum(partial_value, "tensor")
    share_cols = summed.shape[1] // lax.axis_size("tensor")
    own_share = lax.dynamic_slice_in_dim(
        summed, lax.axis_index("tensor") * share_cols, share_cols, 1
    )
    return own_share.astype(jnp.bfloat16).reshape(STEPS, tok_rows, own_share.shape[1])


def solution(mesh):
    return jax.shard_map(
        on_device,
        mesh=mesh,
        in_specs=(
            P(None, ("group", "patch"), None),
            P(None, "tensor"),
            P(None, ("group", "patch"), None, "tensor"),
            P(("group", "patch"), None, "tensor"),
            P(("group", "patch"), None, "tensor"),
            P("tensor", None),
        ),
        out_specs=P(None, ("group", "patch"), "tensor"),
        check_vma=False,
    )
```

profile of v0, /device:TPU:1, one launch (start us, length us, event | category | flops | bytes accessed | tf_op | source)
XLA Modules:
  0.0 143.4 jit_solution(6385953092519611168)
XLA Ops:
  6.5 0.0 copy-start
  6.5 0.0 copy-start.4
  6.5 0.0 all-gather.5.cloned.1.call-start
  6.5 0.8 multiply_exponential_fusion
  7.4 0.1 copy.19
  7.5 0.2 broadcast_in_dim.2
  7.7 0.0 copy-start.3
  7.7 0.1 reshape.13
  7.8 0.0 copy-done.4
  7.8 0.3 fusion.29
  8.1 0.5 copy-done.3
  8.6 0.8 divide_convert_fusion.4
  9.4 0.0 all-gather.5.cloned.1.call-update
  9.4 0.0 all-gather.3.cloned.1.call-start
  9.5 0.7 copy.10
  10.2 0.0 all-gather.3.cloned.1.call-update
  10.2 0.0 copy-done
  10.2 3.2 %fusion.8 = bf16[2,72,768]{2,1,0:T(8,128)(2,1)S(1)} fusion(bf16[2,72,3072]{2,1,0:T(8,128)(2,1)S(1)} %copy-done, bf16[3072,768]{1,0:T(8,128)(2,1)} %param.7), kind=kOutput, calls=%fused_computation.11 | convolution fusion | flops 679587840 | bytes 5824512 | tf_op jit(solution)/shard_map/std,de->ste/dot_general | solution.py:30
  13.5 0.1 reshape_squeeze.22
  13.6 0.1 reshape_squeeze.19
  13.8 43.2 %all-gather.5.cloned.1.call-done = bf16[576,2,768]{2,0,1:T(8,128)(2,1)} async-done(((bf16[72,2,768]{2,0,1:T(8,128)(2,1)}), bf16[576,2,768]{2,0,1:T(8,128)(2,1)}) %all-gather.5.cloned.1.call-update) | async-done | bytes 1769488 | tf_op jit(solution)/shard_map/all_gather | solution.py:41
  57.0 47.2 %all-gather.3.cloned.1.call-done = bf16[576,2,768]{2,0,1:T(8,128)(2,1)} async-done(((bf16[72,2,768]{2,0,1:T(8,128)(2,1)}), bf16[576,2,768]{2,0,1:T(8,128)(2,1)}) %all-gather.3.cloned.1.call-update) | async-done | bytes 1769488 | tf_op jit(solution)/shard_map/all_gather | solution.py:40
  104.3 2.4 %add_convert_fusion = bf16[576,2,768]{2,0,1:T(8,128)(2,1)S(1)} fusion(bf16[576,2,768]{2,0,1:T(8,128)(2,1)} %all-gather.5.cloned.1.call-done, bf16[576,2,768]{2,0,1:T(8,128)(2,1)} %all-gather.3.cloned.1.call-done), kind=kLoop, calls=%fused_computation.4 | loop fusion | flops 3538944 | bytes 5308416 | tf_op jit(solution)/shard_map/convert_element_type | solution.py:42
  106.8 1.0 fusion.28
  107.8 1.5 %copy.22 = bf16[576,1,768]{0,2,1:T(8,128)(2,1)S(1)} copy(bf16[576,1,768]{2,0,1:T(8,128)(2,1)} %get-tuple-element.7) | data formatting | bytes 1769472 | tf_op jit(solution)/shard_map/slice | solution.py:17
  109.3 0.6 fusion.31
  109.9 0.0 copy-start.1
  109.9 1.3 convolution_multiply_fusion
  111.3 0.5 copy-done.1
  111.8 1.3 fusion.27
  113.2 1.5 %copy.13 = bf16[576,1,768]{0,2,1:T(8,128)(2,1)S(1)} copy(bf16[576,1,768]{2,0,1:T(8,128)(2,1)} %get-tuple-element.5) | data formatting | bytes 1769472 | tf_op jit(solution)/shard_map/slice | solution.py:17
  114.7 0.6 fusion.34
  115.3 1.3 convolution_multiply_fusion.1
  116.6 0.6 copy.21
  117.2 0.0 copy-start.2
  117.2 2.5 %fusion.12 = bf16[72,6,128]{2,0,1:T(8,128)(2,1)S(1)} fusion(bf16[576,6,128]{0,2,1:T(8,128)(2,1)S(1)} %bitcast.42, f32[6,72]{1,0:T(8,128)S(1)} %fusion.31, f32[6,72,576]{2,1,0:T(8,128)} %convolution_multiply_fusion), kind=kOutput, calls=%fused_computation.15 | convolution fusion | flops 64503792 | bytes 1992384 | tf_op jit(solution)/shard_map/hqk,khd->qhd/dot_general | solution.py:23
  119.8 0.1 stack_reshape.7
  120.0 0.0 copy-done.2
  120.0 0.6 copy.12
  120.6 2.4 %fusion.11 = bf16[72,6,128]{2,0,1:T(8,128)(2,1)S(1)} fusion(bf16[576,6,128]{0,2,1:T(8,128)(2,1)S(1)} %bitcast.43, f32[6,72]{1,0:T(8,128)S(1)} %fusion.34, f32[6,72,576]{2,1,0:T(8,128)} %convolution_multiply_fusion.1), kind=kOutput, calls=%fused_computation.14 | convolution fusion | flops 64503792 | bytes 1992384 | tf_op jit(solution)/shard_map/hqk,khd->qhd/dot_general | solution.py:23
  123.1 0.1 stack_reshape.6
  123.3 3.2 %fusion.37 = f32[144,3072]{1,0:T(8,128)S(1)} fusion(bf16[144,768]{1,0:T(8,128)(2,1)S(1)} %bitcast.44, bf16[768,3072]{1,0:T(8,128)(2,1)} %param.11), kind=kOutput, calls=%fused_computation.41 | convolution fusion | flops 679477248 | bytes 6709248 | tf_op jit(solution)/shard_map/dot_general | solution.py:52
  126.5 9.2 %all-reduce.1 = bf16[144,3072]{1,0:T(8,128)(2,1)S(1)} all-reduce(f32[144,3072]{1,0:T(8,128)S(1)} %fusion.37), channel_id=1, replica_groups=mesh['group'=2,'patch'=8,'tensor'=2] {'tensor'}, use_global_device_ids=true, to_apply=%region_4.5 | all-reduce | flops 442368 | bytes 2654208 | tf_op jit(solution)/shard_map/psum | solution.py:53
  135.8 0.8 dynamic-slice_convert_fusion
  (6 shorter events, 0.2 us)
Async XLA Ops:
  6.5 3.7 %copy-start = (bf16[2,72,3072]{2,1,0:T(8,128)(2,1)S(1)}, bf16[2,72,3072]{2,1,0:T(8,128)(2,1)}, u32[]{:S(2)}) copy-start(bf16[2,72,3072]{2,1,0:T(8,128)(2,1)} %param.6) | copy-start | bytes 2654212
  6.5 1.3 copy-start.4
  6.5 50.5 %all-gather.5.cloned.1.call-start = ((), (), s32[]{:S(2)}) async-start(), calls=%async_computation.1 | async-start | bytes 1990656 | tf_op jit(solution)/shard_map/all_gather | solution.py:41
  7.7 0.9 copy-start.3
  9.4 94.8 %all-gather.3.cloned.1.call-start = ((), (), s32[]{:S(2)}) async-start(), calls=%async_computation | async-start | bytes 1990656 | tf_op jit(solution)/shard_map/all_gather | solution.py:40
  109.9 1.9 %copy-start.1 = (bf16[576,2,768]{2,0,1:T(8,128)(2,1)S(1)}, bf16[576,2,768]{2,0,1:T(8,128)(2,1)}, u32[]{:S(2)}) copy-start(bf16[576,2,768]{2,0,1:T(8,128)(2,1)} %all-gather.3.cloned.1.call-done) | copy-start | bytes 5308420
  117.2 2.7 %copy-start.2 = (bf16[576,1,768]{2,0,1:T(8,128)(2,1)S(1)}, bf16[576,1,768]{2,0,1:T(8,128)(2,1)}, u32[]{:S(2)}) copy-start(bf16[576,1,768]{2,0,1:T(8,128)(2,1)} %get-tuple-element.6) | copy-start | bytes 2654212
Sparse Core Ops, SparseCore 0:
  9.6 47.3 all-gather.4
  59.3 44.9 all-gather.2
where the time goes:
time: 144 us; the launch traced here: 143 us
  waiting for transfers between devices  90.5 us (63%)
  matrix products  15.2 us (11%)
  between operations  13.6 us (9%)
  local copies, waits for them, and re-layouts  10.7 us (7%)
  blocking collectives  9.25 us (6%)
  other arithmetic  4.05 us (3%)
    all_gather x1, waiting for transfers between devices, on_device(): previous_all = lax.all_gather(prev_kv, 'patch', axis=0, tiled=True)  47.2 us
    all_gather x1, waiting for transfers between devices, on_device(): update_all = lax.all_gather(update, 'patch', axis=0, tiled=True)  43.2 us
    psum x1, blocking collectives, on_device(): summed = lax.psum(partial_value, 'tensor')  9.25 us
    slice x4, local copies, waits for them, and re-layouts, attend(): key_heads = key_table[:, 0].reshape(key_rows, head_count, head_size)  5.42 us
    dot_general x2, matrix products, attend(): jnp.einsum('hqk,khd->qhd', weights, value_heads, preferred_element_type=j...  4.95 us
    dot_general x1, matrix products, on_device(): jnp.dot(flat_rows, w_out, preferred_element_type=jnp.float32)  3.23 us
    dot_general x1, matrix products, on_device(): jnp.einsum('std,de->ste', hidden, w_q, preferred_element_type=jnp.float32)  3.22 us
  transfers between devices with their start and end apart: 2, of which 2 were waited for; matrix products, arithmetic and copies ran while one was open for 3% of the time, Pallas kernels for 0%

commit v1 on v0

v1 whole, which is shorter than its diff:
```python
import functools

import jax
import jax.numpy as jnp
from jax import lax
from jax.experimental import pallas as pl
from jax.experimental.pallas import tpu as pltpu
from jax.sharding import PartitionSpec as P

HD = 128
STEPS = 2
CLIP = 1.0
MESH = pl.DeviceIdType.MESH
F32 = jnp.float32
BF16 = jnp.bfloat16
DOWN, UP, LEFT, RIGHT = 0, 1, 2, 3


def grid_of(count):
    columns = 1
    while columns * columns * 4 <= count and count % (columns * 2) == 0:
        columns *= 2
    return count // columns, columns


def kernel(
    rows, cols,
    hidden, w_q, fresh, prev, exps, w_out,
    out,
    hid, wq, wo_own, wo_far, query, table, copy_own, probs, att, att_far,
    local_sem, send_sem, recv_sem, core_send, core_recv, att_send, att_recv,
):
    tok, width = prev.shape[1], prev.shape[2]
    heads = width // HD
    n = rows * cols
    keys = n * tok
    half = w_out.shape[1] // 2
    me = lax.axis_index("patch")
    core = lax.axis_index("tensor")
    row, col = me // cols, me % cols
    q_parts = wq.shape[0]

    barrier = pltpu.get_barrier_semaphore()
    near = [
        (row > 0, me - cols), (row < rows - 1, me + cols),
        (col > 0, me - 1), (col < cols - 1, me + 1),
    ]
    count = jnp.int32(1)
    for here, index in near:
        @pl.when(here)
        def _(index=index):
            pl.semaphore_signal(barrier, inc=1, device_id={"patch": index}, device_id_type=MESH)
        count = count + here.astype(jnp.int32)
    pl.semaphore_signal(barrier, inc=1, device_id={"tensor": 1 - core}, device_id_type=MESH)

    local = [pltpu.make_async_copy(hidden, hid, local_sem.at[0])]
    part = width // q_parts
    for j in range(q_parts):
        local.append(
            pltpu.make_async_copy(w_q.at[:, pl.ds(j * part, part)], wq.at[j], local_sem.at[1 + j])
        )
    mine = pl.ds(pl.multiple_of(core * half, half), half)
    theirs = pl.ds(pl.multiple_of((1 - core) * half, half), half)
    for copy in local:
        copy.start()
    wo_copy = pltpu.make_async_copy(w_out.at[:, mine], wo_own, local_sem.at[1 + q_parts])
    wo_copy.start()
    pl.semaphore_wait(barrier, count)

    sent = []

    def remote(src, chunk, block, way):
        index = (me - cols, me + cols, me - 1, me + 1)[way]
        return pltpu.make_async_remote_copy(
            src_ref=src, dst_ref=table.at[chunk, block],
            send_sem=send_sem.at[chunk, block, way], recv_sem=recv_sem.at[chunk, block],
            device_id={"patch": index}, device_id_type=MESH,
        )

    def push(src, chunk, block, way, when):
        @pl.when(when)
        def _():
            remote(src, chunk, block, way).start()

    ways_row = ((DOWN, row > 0), (UP, row < rows - 1))
    ways_col = ((LEFT, col > 0), (RIGHT, col < cols - 1))

    def own_src(chunk):
        return prev.at[chunk] if chunk < 2 else copy_own.at[chunk - 2]

    def send_own(chunk):
        for way, when in ways_row + ways_col:
            push(own_src(chunk), chunk, me, way, when)

    def landed(chunk, block):
        remote(table.at[chunk, block], chunk, block, UP).wait_recv()

    def row_events(chunk):
        for d in range(1, rows):
            for way, when, src_row in ((UP, row >= d, row - d), (DOWN, row + d < rows, row + d)):
                @pl.when(when)
                def _(way=way, src_row=src_row):
                    block = src_row * cols + col
                    landed(chunk, block)
                    slot = table.at[chunk, block]
                    for side, ok in ways_col:
                        push(slot, chunk, block, side, ok)
                    push(slot, chunk, block, way, ways_row[way][1])

    def col_events(chunk):
        for e in range(1, cols):
            for k in range(rows):
                for way, when, src_col in ((RIGHT, col >= e, col - e), (LEFT, col + e < cols, col + e)):
                    @pl.when(when)
                    def _(way=way, src_col=src_col, k=k):
                        block = k * cols + src_col
                        landed(chunk, block)
                        if e < cols - 1:
                            push(table.at[chunk, block], chunk, block, way, ways_col[way - 2][1])

    def drain():
        for chunk in range(4):
            for way, when in ways_row + ways_col:
                @pl.when(when)
                def _(way=way, chunk=chunk):
                    remote(own_src(chunk), chunk, me, way).wait_send()
            for d in range(1, rows):
                for way, when, src_row in ((UP, row >= d, row - d), (DOWN, row + d < rows, row + d)):
                    for side, ok in ways_col + (ways_row[way],):
                        @pl.when(jnp.logical_and(when, ok))
                        def _(side=side, src_row=src_row, chunk=chunk):
                            block = src_row * cols + col
                            remote(table.at[chunk, block], chunk, block, side).wait_send()
            for e in range(1, cols - 1):
                for k in range(rows):
                    for way, when, src_col in ((RIGHT, col >= e, col - e), (LEFT, col + e < cols, col + e)):
                        @pl.when(jnp.logical_and(when, ways_col[way - 2][1]))
                        def _(way=way, src_col=src_col, k=k, chunk=chunk):
                            block = k * cols + src_col
                            remote(table.at[chunk, block], chunk, block, way).wait_send()

    send_own(0)
    send_own(1)
    far_copy = pltpu.make_async_remote_copy(
        src_ref=w_out.at[:, theirs], dst_ref=wo_far,
        send_sem=core_send, recv_sem=core_recv,
        device_id={"tensor": 1 - core}, device_id_type=MESH,
    )
    far_copy.start()

    for kv in range(2):
        for h in range(heads):
            at = slice(h * HD, (h + 1) * HD)
            factor = jnp.exp2(-exps[kv, :, h:h + 1].astype(F32))
            old = prev[kv, :, at].astype(F32)
            scaled = jnp.clip((fresh[0, kv, :, at].astype(F32) - old) * factor, -CLIP, CLIP).astype(BF16)
            update = (scaled.astype(F32) / factor).astype(BF16)
            copy_own[kv, :, at] = (old + update.astype(F32)).astype(BF16)
    send_own(2)
    for chunk in range(4):
        table[chunk, me] = fresh[chunk // 2, chunk % 2]

    local[0].wait()
    for j in range(q_parts):
        local[1 + j].wait()
        result = jnp.dot(hid[...], wq[j], preferred_element_type=F32).astype(BF16)
        query[0, :, j * part:(j + 1) * part] = result[:tok]
        query[1, :, j * part:(j + 1) * part] = result[tok:]

    def softmax(step, h):
        at = slice(h * HD, (h + 1) * HD)
        k_rows = table[2 * step, :, :, at].reshape(keys, HD)
        scores = lax.dot_general(
            query[step, :, at], k_rows, (((1,), (1,)), ((), ())), preferred_element_type=F32
        ) * HD ** -0.5
        e = jnp.exp(scores - jnp.max(scores, axis=1, keepdims=True))
        return (e / jnp.sum(e, axis=1, keepdims=True)).astype(BF16)

    def mix_values(step, h, weights):
        at = slice(h * HD, (h + 1) * HD)
        v_rows = table[2 * step + 1, :, :, at].reshape(keys, HD)
        att[step, :, at] = jnp.dot(weights, v_rows, preferred_element_type=F32).astype(BF16)

    def swap(step):
        return pltpu.make_async_remote_copy(
            src_ref=att.at[step], dst_ref=att_far.at[step],
            send_sem=att_send.at[step], recv_sem=att_recv.at[step],
            device_id={"tensor": 1 - core}, device_id_type=MESH,
        )

    tile = 512
    def project(step):
        swap(step).wait_recv()
        for j in range(half // tile):
            at = slice(j * tile, (j + 1) * tile)
            total = jnp.dot(att[step], wo_own[:, at], preferred_element_type=F32)
            total = total + jnp.dot(att_far[step], wo_far[:, at], preferred_element_type=F32)
            out[step, :, at] = total.astype(BF16)

    row_events(0)
    row_events(1)
    send_own(3)
    row_events(2)
    col_events(0)
    col_events(1)
    for h in range(heads):
        mix_values(0, h, softmax(0, h))
    swap(0).start()
    row_events(3)
    wo_copy.wait()
    far_copy.wait()
    col_events(2)
    for h in range(heads):
        probs[h] = softmax(1, h)
    project(0)
    col_events(3)
    for h in range(heads):
        mix_values(1, h, probs[h])
    swap(1).start()
    project(1)
    swap(0).wait_send()
    swap(1).wait_send()
    drain()


def on_device(rows, cols, hidden, w_q, fresh_kv, prev_kv, exps, w_out):
    tok, width = hidden.shape[1], w_q.shape[1]
    depth, half = w_q.shape[0], w_out.shape[1] // 2
    n = rows * cols
    fresh = jnp.transpose(fresh_kv, (0, 2, 1, 3))
    prev = jnp.transpose(prev_kv, (1, 0, 2))
    powers = jnp.transpose(exps, (1, 0, 2))
    q_parts = 3
    vmem = pl.BlockSpec(memory_space=pltpu.VMEM)
    anywhere = pl.BlockSpec(memory_space=pl.ANY)
    dma = pltpu.SemaphoreType.DMA
    return pl.pallas_call(
        functools.partial(kernel, rows, cols),
        out_shape=jax.ShapeDtypeStruct((STEPS, tok, half), BF16),
        in_specs=[anywhere, anywhere, vmem, vmem, vmem, anywhere],
        out_specs=vmem,
        scratch_shapes=[
            pltpu.VMEM((STEPS * tok, depth), BF16),
            pltpu.VMEM((q_parts, depth, width // q_parts), BF16),
            pltpu.VMEM((width, half), BF16),
            pltpu.VMEM((width, half), BF16),
            pltpu.VMEM((STEPS, tok, width), BF16),
            pltpu.VMEM((2 * STEPS, n, tok, width), BF16),
            pltpu.VMEM((2, tok, width), BF16),
            pltpu.VMEM((width // HD, tok, n * tok), BF16),
            pltpu.VMEM((STEPS, tok, width), BF16),
            pltpu.VMEM((STEPS, tok, width), BF16),
            dma((2 + q_parts,)),
            dma((2 * STEPS, n, 4)),
            dma((2 * STEPS, n)),
            dma,
            dma,
            dma((STEPS,)),
            dma((STEPS,)),
        ],
        compiler_params=pltpu.CompilerParams(
            collective_id=0, has_side_effects=True, vmem_limit_bytes=60 * 2**20
        ),
    )(hidden.reshape(STEPS * tok, depth), w_q, fresh, prev, powers, w_out)


def solution(mesh):
    rows, cols = grid_of(mesh.shape["patch"])
    return jax.shard_map(
        functools.partial(on_device, rows, cols),
        mesh=mesh,
        in_specs=(
            P(None, ("group", "patch"), None),
            P(None, "tensor"),
            P(None, ("group", "patch"), None, "tensor"),
            P(("group", "patch"), None, "tensor"),
            P(("group", "patch"), None, "tensor"),
            P("tensor", None),
        ),
        out_specs=P(None, ("group", "patch"), "tensor"),
        check_vma=False,
    )
```

time: 144 us -> 58.3 us (0.40)
  waiting for transfers between devices: 90.5 us -> 0 us
  Pallas kernels: 0 us -> 51.3 us
  matrix products: 15.2 us -> 0 us
  between operations: 13.6 us -> 0.01 us
  blocking collectives: 9.25 us -> 0 us
  other arithmetic: 4.05 us -> 0 us
  local copies, waits for them, and re-layouts: 10.7 us -> 6.69 us
    all_gather x2 -> x0, waiting for transfers between devices: 90.5 us -> none  [the longest x1 47.2 us: on_device(): previous_all = lax.all_gather(prev_kv, 'patch', axis=0, tiled=True)]
    pallas_call x0 -> x1, Pallas kernels: none -> 51.3 us  [on_device(): pl.pallas_call(functools.partial(kernel, rows, cols), out_shape=jax.Shape...]
    dot_general x6 -> x0, matrix products: 14 us -> none  [the longest x2 4.95 us: attend(): jnp.einsum('hqk,khd->qhd', weights, value_heads, preferred_element_type=j...]
    psum x1 -> x0, blocking collectives: 9.25 us -> none  [on_device(): summed = lax.psum(partial_value, 'tensor')]
    slice x8 -> x0, local copies, waits for them, and re-layouts: 7 us -> none  [the longest x4 5.42 us: attend(): key_heads = key_table[:, 0].reshape(key_rows, head_count, head_size)]
    unnamed x11 -> x4, local copies, waits for them, and re-layouts: 1.76 us -> 6.69 us
    convert_element_type x2 -> x0, other arithmetic: 3.22 us -> none  [the longest x1 2.42 us: on_device(): (previous_all.astype(jnp.float32) + update_all.astype(jnp.float32)).astyp...]
  transfers between devices with their start and end apart: 2 -> 0, of which waited for: 2 -> 0; matrix products, arithmetic and copies ran while one was open for 3% -> 0% of each run, Pallas kernels for 0% -> 0%
where the time goes in v1:
time: 58.3 us; the launch traced here: 58 us
  Pallas kernels  51.3 us (88%)
  local copies, waits for them, and re-layouts  6.69 us (11%)
    pallas_call x1, Pallas kernels, on_device(): pl.pallas_call(functools.partial(kernel, rows, cols), out_shape=jax.Shape...  51.3 us
    unnamed x4, local copies, waits for them, and re-layouts  6.69 us

profile of v1, /device:TPU:1, one launch (start us, length us, event | category | flops | bytes accessed | tf_op | source)
XLA Modules:
  0.0 58.0 jit_solution(1394013467282766469)
XLA Ops:
  0.0 1.4 %copy.9 = s32[72,2,6]{2,0,1:T(8,128)} copy(s32[72,2,6]{0,1,2:T(2,128)} %param.10) | data formatting | bytes 6912 | tf_op args[4]
  1.4 1.6 %copy.13 = bf16[72,2,768]{2,0,1:T(8,128)(2,1)} copy(bf16[72,2,768]{2,1,0:T(2,128)(2,1)} %param.9) | data formatting | bytes 442368 | tf_op args[3]
  3.1 1.8 %copy.12 = bf16[2,72,2,768]{3,1,2,0:T(8,128)(2,1)} copy(bf16[2,72,2,768]{3,2,1,0:T(2,128)(2,1)} %param.8) | data formatting | bytes 884736 | tf_op args[2]
  4.9 51.3 %shard_map.64 = bf16[2,72,1536]{2,1,0:T(8,128)(2,1)} custom-call(bf16[144,3072]{1,0:T(8,128)(2,1)} %bitcast.9, bf16[3072,768]{1,0:T(8,128)(2,1)} %w_q.1, bf16[2,2,72,768]{3,2,1,0:T(8,128)(2,1)} %bitcast.8, bf16[2,72,768]{2,1,0:T(8,128)(2,1)} %bitcast.10, s32[2,72,6]{2,1,0:T(8,128)} %bitcast.11, bf16[768,3072]{1,0:T(8,128)(2,1)} %w_out.1), custom_call_target="tpu_custom_call" | custom-call | tf_op jit(solution)/shard_map/pallas_call | solution.py:237
  56.2 1.8 %copy.15 = bf16[2,72,1536]{2,1,0:T(8,128)(2,1)} copy(bf16[2,72,1536]{2,1,0:T(8,128)(2,1)} %shard_map.64) | data formatting | bytes 884736

commit v2 on v1

v2 whole, which is shorter than its diff:
```python
import functools

import jax
import jax.numpy as jnp
from jax import lax
from jax.experimental import pallas as pl
from jax.experimental.pallas import tpu as pltpu
from jax.sharding import PartitionSpec as P

HD = 128
STEPS = 2
CLIP = 1.0
MESH = pl.DeviceIdType.MESH
F32 = jnp.float32
BF16 = jnp.bfloat16
DOWN, UP = 0, 1


def grid_of(count):
    columns = 1
    while columns * columns * 4 <= count and count % (columns * 2) == 0:
        columns *= 2
    return count // columns, columns


def kernel(
    rows, cols,
    hidden, w_q, fresh, prev, exps, w_out,
    out,
    hid, wq, wo_own, wo_far, query, query_in, table, probs, own_sum, own_stat,
    part_out, stat_out, part_in, stat_in, att, att_far,
    local_sem, send_sem, recv_sem, core_send, core_recv, att_send, att_recv,
    query_send, query_recv, part_send, part_recv, stat_send, stat_recv,
):
    tok, width = prev.shape[1], prev.shape[2]
    heads = width // HD
    keys = rows * tok
    half = w_out.shape[1] // 2
    me = lax.axis_index("patch")
    core = lax.axis_index("tensor")
    row, col = me // cols, me % cols
    q_parts = wq.shape[0]
    peers = range(1, cols)

    def peer(j):
        return row * cols + lax.rem(col + j + cols, cols)

    barrier = pltpu.get_barrier_semaphore()
    count = jnp.int32(cols)
    for here, index in ((row > 0, me - cols), (row < rows - 1, me + cols)):
        @pl.when(here)
        def _(index=index):
            pl.semaphore_signal(barrier, inc=1, device_id={"patch": index}, device_id_type=MESH)
        count = count + here.astype(jnp.int32)
    for j in peers:
        pl.semaphore_signal(barrier, inc=1, device_id={"patch": peer(j)}, device_id_type=MESH)
    pl.semaphore_signal(barrier, inc=1, device_id={"tensor": 1 - core}, device_id_type=MESH)

    local = [pltpu.make_async_copy(hidden, hid, local_sem.at[0])]
    part = width // q_parts
    for j in range(q_parts):
        local.append(
            pltpu.make_async_copy(w_q.at[:, pl.ds(j * part, part)], wq.at[j], local_sem.at[1 + j])
        )
    mine = pl.ds(pl.multiple_of(core * half, half), half)
    theirs = pl.ds(pl.multiple_of((1 - core) * half, half), half)
    for copy in local:
        copy.start()
    wo_copy = pltpu.make_async_copy(w_out.at[:, mine], wo_own, local_sem.at[1 + q_parts])
    wo_copy.start()
    pl.semaphore_wait(barrier, count)

    def remote(src, chunk, src_row, way):
        to = row + (-1, 1)[way]
        slot = lax.rem(src_row - to + 2 * rows, rows)
        return pltpu.make_async_remote_copy(
            src_ref=src, dst_ref=table.at[chunk, slot],
            send_sem=send_sem.at[chunk, lax.rem(src_row - row + rows, rows), way],
            recv_sem=recv_sem.at[chunk, slot],
            device_id={"patch": to * cols + col}, device_id_type=MESH,
        )

    may = (row > 0, row < rows - 1)

    def own_src(chunk):
        return prev.at[chunk] if chunk < 2 else table.at[chunk, rows]

    def send_own(chunk):
        for way in (DOWN, UP):
            @pl.when(may[way])
            def _(way=way):
                remote(own_src(chunk), chunk, row, way).start()

    def sides(d):
        return ((UP, row >= d, -d % rows, row - d), (DOWN, row + d < rows, d, row + d))

    def row_events(chunk, distances):
        for d in distances:
            for way, when, slot, src_row in sides(d):
                @pl.when(when)
                def _(way=way, slot=slot, src_row=src_row):
                    here = table.at[chunk, slot]
                    pltpu.make_async_remote_copy(
                        src_ref=here, dst_ref=here,
                        send_sem=send_sem.at[chunk, slot, way], recv_sem=recv_sem.at[chunk, slot],
                        device_id={"patch": me}, device_id_type=MESH,
                    ).wait_recv()

                    @pl.when(may[way])
                    def _():
                        remote(here, chunk, src_row, way).start()

    def drain():
        for chunk in range(2 * STEPS):
            for way in (DOWN, UP):
                @pl.when(may[way])
                def _(way=way, chunk=chunk):
                    remote(own_src(chunk), chunk, row, way).wait_send()
            for d in range(1, rows):
                for way, when, slot, src_row in sides(d):
                    @pl.when(jnp.logical_and(when, may[way]))
                    def _(way=way, slot=slot, src_row=src_row, chunk=chunk):
                        remote(table.at[chunk, slot], chunk, src_row, way).wait_send()

    send_own(0)
    send_own(1)
    far_copy = pltpu.make_async_remote_copy(
        src_ref=w_out.at[:, theirs], dst_ref=wo_far,
        send_sem=core_send, recv_sem=core_recv,
        device_id={"tensor": 1 - core}, device_id_type=MESH,
    )
    far_copy.start()

    for kv in range(2):
        table[kv, rows] = prev[kv]
        for h in range(heads):
            at = slice(h * HD, (h + 1) * HD)
            factor = jnp.exp2(-exps[kv, :, h:h + 1].astype(F32))
            old = prev[kv, :, at].astype(F32)
            scaled = jnp.clip((fresh[0, kv, :, at].astype(F32) - old) * factor, -CLIP, CLIP).astype(BF16)
            update = (scaled.astype(F32) / factor).astype(BF16)
            table[2 + kv, rows, :, at] = (old + update.astype(F32)).astype(BF16)
    send_own(2)
    for chunk in range(2 * STEPS):
        table[chunk, 0] = fresh[chunk // 2, chunk % 2]

    local[0].wait()
    for j in range(q_parts):
        local[1 + j].wait()
        result = jnp.dot(hid[...], wq[j], preferred_element_type=F32).astype(BF16)
        query[0, :, j * part:(j + 1) * part] = result[:tok]
        query[1, :, j * part:(j + 1) * part] = result[tok:]

    def query_copy(j):
        return pltpu.make_async_remote_copy(
            src_ref=query, dst_ref=query_in.at[j], send_sem=query_send.at[j], recv_sem=query_recv.at[j],
            device_id={"patch": peer(j)}, device_id_type=MESH,
        )

    def part_copies(step, j):
        return [
            pltpu.make_async_remote_copy(
                src_ref=src.at[step, j], dst_ref=dst.at[step, j],
                send_sem=send.at[step, j], recv_sem=recv.at[step, j],
                device_id={"patch": peer(-j)}, device_id_type=MESH,
            )
            for src, dst, send, recv in (
                (part_out, part_in, part_send, part_recv), (stat_out, stat_in, stat_send, stat_recv),
            )
        ]

    for j in peers:
        query_copy(j).start()

    def at_head(h):
        return slice(h * HD, (h + 1) * HD)

    def weigh(step, h, j):
        first = 1 if j else 0
        queries = query_in[j, step, :, at_head(h)] if j else query[step, :, at_head(h)]
        k_rows = table[2 * step, first:first + rows, :, at_head(h)].reshape(keys, HD)
        scores = lax.dot_general(
            queries, k_rows, (((1,), (1,)), ((), ())), preferred_element_type=F32
        ) * HD ** -0.5
        top = jnp.max(scores, axis=1, keepdims=True)
        e = jnp.exp(scores - top)
        probs[j, h] = e.astype(BF16)
        total = jnp.sum(e, axis=1, keepdims=True)
        if j:
            stat_out[step, j, :, h:h + 1] = top
            stat_out[step, j, :, heads + h:heads + h + 1] = total
        else:
            own_stat[:, h:h + 1] = top
            own_stat[:, heads + h:heads + h + 1] = total

    def mix_values(step, h, j):
        first = 1 if j else 0
        v_rows = table[2 * step + 1, first:first + rows, :, at_head(h)].reshape(keys, HD)
        mixed = jnp.dot(probs[j, h], v_rows, preferred_element_type=F32)
        if j:
            total = stat_out[step, j, :, heads + h:heads + h + 1]
            part_out[step, j, :, at_head(h)] = (mixed / total).astype(BF16)
        else:
            own_sum[:, at_head(h)] = mixed

    def each_head(run, step, who):
        for j in who:
            for h in range(heads):
                run(step, h, j)

    def give_back(step):
        for j in peers:
            for copy in part_copies(step, j):
                copy.start()

    def merge(step):
        for j in peers:
            for copy in part_copies(step, j):
                copy.wait_recv()
        for h in range(heads):
            one, two = slice(h, h + 1), slice(heads + h, heads + h + 1)
            top = own_stat[:, one]
            for j in peers:
                top = jnp.maximum(top, stat_in[step, j, :, one])
            share = jnp.exp(own_stat[:, one] - top)
            below = own_stat[:, two] * share
            above = own_sum[:, at_head(h)] * share
            for j in peers:
                share = stat_in[step, j, :, two] * jnp.exp(stat_in[step, j, :, one] - top)
                below = below + share
                above = above + part_in[step, j, :, at_head(h)].astype(F32) * share
            att[step, :, at_head(h)] = (above / below).astype(BF16)

    def swap(step):
        return pltpu.make_async_remote_copy(
            src_ref=att.at[step], dst_ref=att_far.at[step],
            send_sem=att_send.at[step], recv_sem=att_recv.at[step],
            device_id={"tensor": 1 - core}, device_id_type=MESH,
        )

    tile = 512

    def project(step):
        swap(step).wait_recv()
        for j in range(half // tile):
            at = slice(j * tile, (j + 1) * tile)
            total = jnp.dot(att[step], wo_own[:, at], preferred_element_type=F32)
            total = total + jnp.dot(att_far[step], wo_far[:, at], preferred_element_type=F32)
            out[step, :, at] = total.astype(BF16)

    every = range(1, rows)
    row_events(0, every)
    send_own(3)
    row_events(1, every)
    for j in peers:
        query_copy(j).wait_recv()
    each_head(weigh, 0, peers)
    each_head(mix_values, 0, peers)
    give_back(0)
    row_events(2, every)
    each_head(weigh, 0, (0,))
    each_head(mix_values, 0, (0,))
    row_events(3, every[:1])
    merge(0)
    swap(0).start()
    each_head(weigh, 1, peers)
    row_events(3, every[1:2])
    each_head(weigh, 1, (0,))
    wo_copy.wait()
    far_copy.wait()
    project(0)
    row_events(3, every[2:])
    each_head(mix_values, 1, peers)
    give_back(1)
    each_head(mix_values, 1, (0,))
    merge(1)
    swap(1).start()
    project(1)
    for step in range(STEPS):
        swap(step).wait_send()
        for j in peers:
            for copy in part_copies(step, j):
                copy.wait_send()
    for j in peers:
        query_copy(j).wait_send()
    drain()


def on_device(rows, cols, hidden, w_q, fresh_kv, prev_kv, exps, w_out):
    tok, width = hidden.shape[1], w_q.shape[1]
    depth, half = w_q.shape[0], w_out.shape[1] // 2
    heads = width // HD
    fresh = jnp.transpose(fresh_kv, (0, 2, 1, 3))
    prev = jnp.transpose(prev_kv, (1, 0, 2))
    powers = jnp.transpose(exps, (1, 0, 2))
    q_parts = 3
    vmem = pl.BlockSpec(memory_space=pltpu.VMEM)
    anywhere = pl.BlockSpec(memory_space=pl.ANY)
    dma = pltpu.SemaphoreType.DMA
    return pl.pallas_call(
        functools.partial(kernel, rows, cols),
        out_shape=jax.ShapeDtypeStruct((STEPS, tok, half), BF16),
        in_specs=[anywhere, anywhere, vmem, vmem, vmem, anywhere],
        out_specs=vmem,
        scratch_shapes=[
            pltpu.VMEM((STEPS * tok, depth), BF16),
            pltpu.VMEM((q_parts, depth, width // q_parts), BF16),
            pltpu.VMEM((width, half), BF16),
            pltpu.VMEM((width, half), BF16),
            pltpu.VMEM((STEPS, tok, width), BF16),
            pltpu.VMEM((cols, STEPS, tok, width), BF16),
            pltpu.VMEM((2 * STEPS, rows + 1, tok, width), BF16),
            pltpu.VMEM((cols, heads, tok, rows * tok), BF16),
            pltpu.VMEM((tok, width), F32),
            pltpu.VMEM((tok, HD), F32),
            pltpu.VMEM((STEPS, cols, tok, width), BF16),
            pltpu.VMEM((STEPS, cols, tok, HD), F32),
            pltpu.VMEM((STEPS, cols, tok, width), BF16),
            pltpu.VMEM((STEPS, cols, tok, HD), F32),
            pltpu.VMEM((STEPS, tok, width), BF16),
            pltpu.VMEM((STEPS, tok, width), BF16),
            dma((2 + q_parts,)),
            dma((2 * STEPS, rows, 2)),
            dma((2 * STEPS, rows)),
            dma,
            dma,
            dma((STEPS,)),
            dma((STEPS,)),
            dma((cols,)),
            dma((cols,)),
            dma((STEPS, cols)),
            dma((STEPS, cols)),
            dma((STEPS, cols)),
            dma((STEPS, cols)),
        ],
        compiler_params=pltpu.CompilerParams(
            collective_id=0, has_side_effects=True, vmem_limit_bytes=60 * 2**20
        ),
    )(hidden.reshape(STEPS * tok, depth), w_q, fresh, prev, powers, w_out)


def solution(mesh):
    rows, cols = grid_of(mesh.shape["patch"])
    return jax.shard_map(
        functools.partial(on_device, rows, cols),
        mesh=mesh,
        in_specs=(
            P(None, ("group", "patch"), None),
            P(None, "tensor"),
            P(None, ("group", "patch"), None, "tensor"),
            P(("group", "patch"), None, "tensor"),
            P(("group", "patch"), None, "tensor"),
            P("tensor", None),
        ),
        out_specs=P(None, ("group", "patch"), "tensor"),
        check_vma=False,
    )
```

time: 58.3 us -> 53.1 us (0.911)
  Pallas kernels: 51.3 us -> 46.1 us
    pallas_call x1, Pallas kernels: 51.3 us -> 46.1 us  [on_device(): pl.pallas_call(functools.partial(kernel, rows, cols), out_shape=jax.Shape...]
where the time goes in v2:
time: 53.1 us; the launch traced here: 52.8 us
  Pallas kernels  46.1 us (87%)
  local copies, waits for them, and re-layouts  6.69 us (13%)
    pallas_call x1, Pallas kernels, on_device(): pl.pallas_call(functools.partial(kernel, rows, cols), out_shape=jax.Shape...  46.1 us
    unnamed x4, local copies, waits for them, and re-layouts  6.69 us

profile of v2, /device:TPU:1, one launch (start us, length us, event | category | flops | bytes accessed | tf_op | source)
XLA Modules:
  0.0 52.8 jit_solution(18280056578243808666)
XLA Ops:
  0.0 1.4 %copy.9 = s32[72,2,6]{2,0,1:T(8,128)} copy(s32[72,2,6]{0,1,2:T(2,128)} %param.10) | data formatting | bytes 6912 | tf_op args[4]
  1.4 1.6 %copy.13 = bf16[72,2,768]{2,0,1:T(8,128)(2,1)} copy(bf16[72,2,768]{2,1,0:T(2,128)(2,1)} %param.9) | data formatting | bytes 442368 | tf_op args[3]
  3.1 1.8 %copy.12 = bf16[2,72,2,768]{3,1,2,0:T(8,128)(2,1)} copy(bf16[2,72,2,768]{3,2,1,0:T(2,128)(2,1)} %param.8) | data formatting | bytes 884736 | tf_op args[2]
  4.9 46.1 %shard_map.64 = bf16[2,72,1536]{2,1,0:T(8,128)(2,1)} custom-call(bf16[144,3072]{1,0:T(8,128)(2,1)} %bitcast.9, bf16[3072,768]{1,0:T(8,128)(2,1)} %w_q.1, bf16[2,2,72,768]{3,2,1,0:T(8,128)(2,1)} %bitcast.8, bf16[2,72,768]{2,1,0:T(8,128)(2,1)} %bitcast.10, s32[2,72,6]{2,1,0:T(8,128)} %bitcast.11, bf16[768,3072]{1,0:T(8,128)(2,1)} %w_out.1), custom_call_target="tpu_custom_call" | custom-call | tf_op jit(solution)/shard_map/pallas_call | solution.py:300
  51.0 1.8 %copy.15 = bf16[2,72,1536]{2,1,0:T(8,128)(2,1)} copy(bf16[2,72,1536]{2,1,0:T(8,128)(2,1)} %shard_map.64) | data formatting | bytes 884736

commit v3 on v2

v3 whole, which is shorter than its diff:
```python
import functools

import jax
import jax.numpy as jnp
from jax import lax
from jax.experimental import pallas as pl
from jax.experimental.pallas import tpu as pltpu
from jax.sharding import PartitionSpec as P

HD = 128
STEPS = 2
CLIP = 1.0
MESH = pl.DeviceIdType.MESH
F32 = jnp.float32
BF16 = jnp.bfloat16
QUAD = 4
BY_ROW = ()


def grid_of(count):
    columns = 1
    while columns * columns * 4 <= count and count % (columns * 2) == 0:
        columns *= 2
    return count // columns, columns


def kernel(
    rows, cols,
    hidden, w_q, fresh, prev, exps, w_out,
    out,
    hid, wq, wo_own, wo_far, query, query_in, table, probs, own_sum, own_stat,
    part_out, stat_out, part_in, stat_in, att, att_far,
    local_sem, send_sem, recv_sem, core_send, core_recv, att_send, att_recv,
    query_send, query_recv, part_send, part_recv, stat_send, stat_recv,
):
    tok, width = prev.shape[1], prev.shape[2]
    heads = width // HD
    keys = QUAD * tok
    half = w_out.shape[1] // 2
    me = lax.axis_index("patch")
    core = lax.axis_index("tensor")
    row, col = me // cols, me % cols
    q_parts = wq.shape[0]
    groups = rows * cols // QUAD
    peers = range(1, groups)
    group = (row // 2) * (cols // 2) + col // 2
    row_peer = (row + 1 - 2 * (row % 2)) * cols + col
    col_peer = row * cols + col + 1 - 2 * (col % 2)

    def peer(j):
        to = lax.rem(group + j + groups, groups)
        return (2 * (to // (cols // 2)) + row % 2) * cols + 2 * (to % (cols // 2)) + col % 2

    barrier = pltpu.get_barrier_semaphore()
    for index in [row_peer, col_peer] + [peer(j) for j in peers]:
        pl.semaphore_signal(barrier, inc=1, device_id={"patch": index}, device_id_type=MESH)
    pl.semaphore_signal(barrier, inc=1, device_id={"tensor": 1 - core}, device_id_type=MESH)

    local = [pltpu.make_async_copy(hidden, hid, local_sem.at[0])]
    part = width // q_parts
    for j in range(q_parts):
        local.append(
            pltpu.make_async_copy(w_q.at[:, pl.ds(j * part, part)], wq.at[j], local_sem.at[1 + j])
        )
    mine = pl.ds(pl.multiple_of(core * half, half), half)
    theirs = pl.ds(pl.multiple_of((1 - core) * half, half), half)
    for copy in local:
        copy.start()
    wo_copy = pltpu.make_async_copy(w_out.at[:, mine], wo_own, local_sem.at[1 + q_parts])
    wo_copy.start()
    pl.semaphore_wait(barrier, groups + 2)

    def remote(src, chunk, slot, index):
        return pltpu.make_async_remote_copy(
            src_ref=src, dst_ref=table.at[chunk, slot],
            send_sem=send_sem.at[chunk, slot], recv_sem=recv_sem.at[chunk, slot],
            device_id={"patch": index}, device_id_type=MESH,
        )

    def own_copies(chunk):
        src = prev.at[chunk] if chunk < 2 else table.at[chunk, QUAD]
        return [remote(src, chunk, 2, col_peer), remote(src, chunk, 1, row_peer)]

    def onward(chunk):
        first, index = (2, row_peer) if chunk in BY_ROW else (1, col_peer)
        return first, remote(table.at[chunk, first], chunk, 3, index)

    def send_own(chunk):
        for copy in own_copies(chunk):
            copy.start()

    def forward(chunk):
        first, copy = onward(chunk)
        own_copies(chunk)[2 - first].wait_recv()
        copy.start()

    def complete(chunk):
        first, copy = onward(chunk)
        own_copies(chunk)[first - 1].wait_recv()
        copy.wait_recv()

    def drain():
        for chunk in range(2 * STEPS):
            for copy in own_copies(chunk) + [onward(chunk)[1]]:
                copy.wait_send()

    send_own(0)
    send_own(1)
    far_copy = pltpu.make_async_remote_copy(
        src_ref=w_out.at[:, theirs], dst_ref=wo_far,
        send_sem=core_send, recv_sem=core_recv,
        device_id={"tensor": 1 - core}, device_id_type=MESH,
    )
    far_copy.start()

    def query_copy(j):
        return pltpu.make_async_remote_copy(
            src_ref=query, dst_ref=query_in.at[j], send_sem=query_send.at[j], recv_sem=query_recv.at[j],
            device_id={"patch": peer(j)}, device_id_type=MESH,
        )

    def part_copies(step, j):
        return [
            pltpu.make_async_remote_copy(
                src_ref=src.at[step, j], dst_ref=dst.at[step, j],
                send_sem=send.at[step, j], recv_sem=recv.at[step, j],
                device_id={"patch": peer(-j)}, device_id_type=MESH,
            )
            for src, dst, send, recv in (
                (part_out, part_in, part_send, part_recv), (stat_out, stat_in, stat_send, stat_recv),
            )
        ]

    local[0].wait()
    for j in range(q_parts):
        local[1 + j].wait()
        result = jnp.dot(hid[...], wq[j], preferred_element_type=F32).astype(BF16)
        query[0, :, j * part:(j + 1) * part] = result[:tok]
        query[1, :, j * part:(j + 1) * part] = result[tok:]

    for j in peers:
        query_copy(j).start()

    for kv in range(2):
        table[kv, QUAD] = prev[kv]
        for h in range(heads):
            at = slice(h * HD, (h + 1) * HD)
            factor = jnp.exp2(-exps[kv, :, h:h + 1].astype(F32))
            old = prev[kv, :, at].astype(F32)
            scaled = jnp.clip((fresh[0, kv, :, at].astype(F32) - old) * factor, -CLIP, CLIP).astype(BF16)
            update = (scaled.astype(F32) / factor).astype(BF16)
            table[2 + kv, QUAD, :, at] = (old + update.astype(F32)).astype(BF16)
    for chunk in range(2 * STEPS):
        table[chunk, 0] = fresh[chunk // 2, chunk % 2]

    def at_head(h):
        return slice(h * HD, (h + 1) * HD)

    def weigh(step, h, j):
        other = not isinstance(j, int) or j > 0
        first = 1 if other else 0
        queries = query_in[j, step, :, at_head(h)] if other else query[step, :, at_head(h)]
        k_rows = table[2 * step, first:first + QUAD, :, at_head(h)].reshape(keys, HD)
        scores = lax.dot_general(
            queries, k_rows, (((1,), (1,)), ((), ())), preferred_element_type=F32
        ) * HD ** -0.5
        top = jnp.max(scores, axis=1, keepdims=True)
        e = jnp.exp(scores - top)
        probs[j, h] = e.astype(BF16)
        total = jnp.sum(e, axis=1, keepdims=True)
        if other:
            stat_out[step, j, :, h:h + 1] = top
            stat_out[step, j, :, heads + h:heads + h + 1] = total
        else:
            own_stat[:, h:h + 1] = top
            own_stat[:, heads + h:heads + h + 1] = total

    def mix_values(step, h, j):
        other = not isinstance(j, int) or j > 0
        first = 1 if other else 0
        v_rows = table[2 * step + 1, first:first + QUAD, :, at_head(h)].reshape(keys, HD)
        mixed = jnp.dot(probs[j, h], v_rows, preferred_element_type=F32)
        if other:
            total = stat_out[step, j, :, heads + h:heads + h + 1]
            part_out[step, j, :, at_head(h)] = (mixed / total).astype(BF16)
        else:
            own_sum[:, at_head(h)] = mixed

    def each_head(run, step, who):
        for j in who:
            for h in range(heads):
                run(step, h, j)

    def each_peer(runs, step):
        def body(j, carry):
            for run in runs:
                for h in range(heads):
                    run(step, h, j)
            return carry
        if groups == 2:
            body(1, 0)
        else:
            lax.fori_loop(1, groups, body, 0)

    def give_back(step):
        for j in peers:
            for copy in part_copies(step, j):
                copy.start()

    def merge(step):
        for j in peers:
            for copy in part_copies(step, j):
                copy.wait_recv()
        for h in range(heads):
            one, two = slice(h, h + 1), slice(heads + h, heads + h + 1)
            top = own_stat[:, one]
            for j in peers:
                top = jnp.maximum(top, stat_in[step, j, :, one])
            share = jnp.exp(own_stat[:, one] - top)
            below = own_stat[:, two] * share
            above = own_sum[:, at_head(h)] * share
            for j in peers:
                share = stat_in[step, j, :, two] * jnp.exp(stat_in[step, j, :, one] - top)
                below = below + share
                above = above + part_in[step, j, :, at_head(h)].astype(F32) * share
            att[step, :, at_head(h)] = (above / below).astype(BF16)

    def swap(step):
        return pltpu.make_async_remote_copy(
            src_ref=att.at[step], dst_ref=att_far.at[step],
            send_sem=att_send.at[step], recv_sem=att_recv.at[step],
            device_id={"tensor": 1 - core}, device_id_type=MESH,
        )

    tile = 512

    def project(step):
        swap(step).wait_recv()
        for j in range(half // tile):
            at = slice(j * tile, (j + 1) * tile)
            total = jnp.dot(att[step], wo_own[:, at], preferred_element_type=F32)
            total = total + jnp.dot(att_far[step], wo_far[:, at], preferred_element_type=F32)
            out[step, :, at] = total.astype(BF16)

    forward(0)
    send_own(2)
    forward(1)
    send_own(3)
    forward(2)
    complete(0)
    complete(1)
    for j in peers:
        query_copy(j).wait_recv()
    each_peer((weigh, mix_values), 0)
    give_back(0)
    forward(3)
    complete(2)
    each_peer((weigh,), 1)
    complete(3)
    each_peer((mix_values,), 1)
    give_back(1)
    each_head(weigh, 0, (0,))
    each_head(mix_values, 0, (0,))
    wo_copy.wait()
    far_copy.wait()
    merge(0)
    swap(0).start()
    each_head(weigh, 1, (0,))
    each_head(mix_values, 1, (0,))
    project(0)
    merge(1)
    swap(1).start()
    project(1)
    for step in range(STEPS):
        swap(step).wait_send()
        for j in peers:
            for copy in part_copies(step, j):
                copy.wait_send()
    for j in peers:
        query_copy(j).wait_send()
    drain()


def on_device(rows, cols, hidden, w_q, fresh_kv, prev_kv, exps, w_out):
    tok, width = hidden.shape[1], w_q.shape[1]
    depth, half = w_q.shape[0], w_out.shape[1] // 2
    heads = width // HD
    groups = rows * cols // QUAD
    fresh = jnp.transpose(fresh_kv, (0, 2, 1, 3))
    prev = jnp.transpose(prev_kv, (1, 0, 2))
    powers = jnp.transpose(exps, (1, 0, 2))
    q_parts = 3
    vmem = pl.BlockSpec(memory_space=pltpu.VMEM)
    anywhere = pl.BlockSpec(memory_space=pl.ANY)
    dma = pltpu.SemaphoreType.DMA
    return pl.pallas_call(
        functools.partial(kernel, rows, cols),
        out_shape=jax.ShapeDtypeStruct((STEPS, tok, half), BF16),
        in_specs=[anywhere, anywhere, vmem, vmem, vmem, anywhere],
        out_specs=vmem,
        scratch_shapes=[
            pltpu.VMEM((STEPS * tok, depth), BF16),
            pltpu.VMEM((q_parts, depth, width // q_parts), BF16),
            pltpu.VMEM((width, half), BF16),
            pltpu.VMEM((width, half), BF16),
            pltpu.VMEM((STEPS, tok, width), BF16),
            pltpu.VMEM((groups, STEPS, tok, width), BF16),
            pltpu.VMEM((2 * STEPS, QUAD + 1, tok, width), BF16),
            pltpu.VMEM((groups, heads, tok, QUAD * tok), BF16),
            pltpu.VMEM((tok, width), F32),
            pltpu.VMEM((tok, HD), F32),
            pltpu.VMEM((STEPS, groups, tok, width), BF16),
            pltpu.VMEM((STEPS, groups, tok, HD), F32),
            pltpu.VMEM((STEPS, groups, tok, width), BF16),
            pltpu.VMEM((STEPS, groups, tok, HD), F32),
            pltpu.VMEM((STEPS, tok, width), BF16),
            pltpu.VMEM((STEPS, tok, width), BF16),
            dma((2 + q_parts,)),
            dma((2 * STEPS, QUAD)),
            dma((2 * STEPS, QUAD)),
            dma,
            dma,
            dma((STEPS,)),
            dma((STEPS,)),
            dma((groups,)),
            dma((groups,)),
            dma((STEPS, groups)),
            dma((STEPS, groups)),
            dma((STEPS, groups)),
            dma((STEPS, groups)),
        ],
        compiler_params=pltpu.CompilerParams(
            collective_id=0, has_side_effects=True, vmem_limit_bytes=60 * 2**20
        ),
    )(hidden.reshape(STEPS * tok, depth), w_q, fresh, prev, powers, w_out)


def solution(mesh):
    rows, cols = grid_of(mesh.shape["patch"])
    return jax.shard_map(
        functools.partial(on_device, rows, cols),
        mesh=mesh,
        in_specs=(
            P(None, ("group", "patch"), None),
            P(None, "tensor"),
            P(None, ("group", "patch"), None, "tensor"),
            P(("group", "patch"), None, "tensor"),
            P(("group", "patch"), None, "tensor"),
            P("tensor", None),
        ),
        out_specs=P(None, ("group", "patch"), "tensor"),
        check_vma=False,
    )
```

time: 53.1 us -> 45.3 us (0.85)
  Pallas kernels: 46.1 us -> 38.3 us
    pallas_call x1, Pallas kernels: 46.1 us -> 38.3 us  [on_device(): pl.pallas_call(functools.partial(kernel, rows, cols), out_shape=jax.Shape...]
where the time goes in v3:
time: 45.3 us; the launch traced here: 45 us
  Pallas kernels  38.3 us (85%)
  local copies, waits for them, and re-layouts  6.69 us (15%)
    pallas_call x1, Pallas kernels, on_device(): pl.pallas_call(functools.partial(kernel, rows, cols), out_shape=jax.Shape...  38.3 us
    unnamed x4, local copies, waits for them, and re-layouts  6.69 us

profile of v3, /device:TPU:1, one launch (start us, length us, event | category | flops | bytes accessed | tf_op | source)
XLA Modules:
  0.0 45.0 jit_solution(8688993633597451145)
XLA Ops:
  0.0 1.4 %copy.9 = s32[72,2,6]{2,0,1:T(8,128)} copy(s32[72,2,6]{0,1,2:T(2,128)} %param.10) | data formatting | bytes 6912 | tf_op args[4]
  1.4 1.6 %copy.13 = bf16[72,2,768]{2,0,1:T(8,128)(2,1)} copy(bf16[72,2,768]{2,1,0:T(2,128)(2,1)} %param.9) | data formatting | bytes 442368 | tf_op args[3]
  3.1 1.8 %copy.12 = bf16[2,72,2,768]{3,1,2,0:T(8,128)(2,1)} copy(bf16[2,72,2,768]{3,2,1,0:T(2,128)(2,1)} %param.8) | data formatting | bytes 884736 | tf_op args[2]
  4.9 38.3 %shard_map.64 = bf16[2,72,1536]{2,1,0:T(8,128)(2,1)} custom-call(bf16[144,3072]{1,0:T(8,128)(2,1)} %bitcast.9, bf16[3072,768]{1,0:T(8,128)(2,1)} %w_q.1, bf16[2,2,72,768]{3,2,1,0:T(8,128)(2,1)} %bitcast.8, bf16[2,72,768]{2,1,0:T(8,128)(2,1)} %bitcast.10, s32[2,72,6]{2,1,0:T(8,128)} %bitcast.11, bf16[768,3072]{1,0:T(8,128)(2,1)} %w_out.1), custom_call_target="tpu_custom_call" | custom-call | tf_op jit(solution)/shard_map/pallas_call | solution.py:296
  43.2 1.8 %copy.15 = bf16[2,72,1536]{2,1,0:T(8,128)(2,1)} copy(bf16[2,72,1536]{2,1,0:T(8,128)(2,1)} %shard_map.64) | data formatting | bytes 884736

commit v4 on v3

--- a/solution.py
+++ b/solution.py
@@ -33,7 +33,7 @@
     local_sem, send_sem, recv_sem, core_send, core_recv, att_send, att_recv,
     query_send, query_recv, part_send, part_recv, stat_send, stat_recv,
 ):
-    tok, width = prev.shape[1], prev.shape[2]
+    tok, width = prev.shape[0], prev.shape[2]
     heads = width // HD
     keys = QUAD * tok
     half = w_out.shape[1] // 2
@@ -78,7 +78,7 @@
         )
 
     def own_copies(chunk):
-        src = prev.at[chunk] if chunk < 2 else table.at[chunk, QUAD]
+        src = table.at[chunk, QUAD]
         return [remote(src, chunk, 2, col_peer), remote(src, chunk, 1, row_peer)]
 
     def onward(chunk):
@@ -104,8 +104,9 @@
             for copy in own_copies(chunk) + [onward(chunk)[1]]:
                 copy.wait_send()
 
-    send_own(0)
-    send_own(1)
+    for kv in range(2):
+        table[kv, QUAD] = prev[:, kv, :]
+        send_own(kv)
     far_copy = pltpu.make_async_remote_copy(
         src_ref=w_out.at[:, theirs], dst_ref=wo_far,
         send_sem=core_send, recv_sem=core_recv,
@@ -141,17 +142,17 @@
     for j in peers:
         query_copy(j).start()
 
+    for chunk in range(2 * STEPS):
+        table[chunk, 0] = fresh[chunk // 2, :, chunk % 2, :]
     for kv in range(2):
-        table[kv, QUAD] = prev[kv]
+        factors = jnp.exp2(-exps[:, kv, :].astype(F32)).T
         for h in range(heads):
             at = slice(h * HD, (h + 1) * HD)
-            factor = jnp.exp2(-exps[kv, :, h:h + 1].astype(F32))
-            old = prev[kv, :, at].astype(F32)
-            scaled = jnp.clip((fresh[0, kv, :, at].astype(F32) - old) * factor, -CLIP, CLIP).astype(BF16)
+            factor = factors[:, h:h + 1]
+            old = table[kv, QUAD, :, at].astype(F32)
+            scaled = jnp.clip((table[kv, 0, :, at].astype(F32) - old) * factor, -CLIP, CLIP).astype(BF16)
             update = (scaled.astype(F32) / factor).astype(BF16)
             table[2 + kv, QUAD, :, at] = (old + update.astype(F32)).astype(BF16)
-    for chunk in range(2 * STEPS):
-        table[chunk, 0] = fresh[chunk // 2, chunk % 2]
 
     def at_head(h):
         return slice(h * HD, (h + 1) * HD)
@@ -286,9 +287,7 @@
     depth, half = w_q.shape[0], w_out.shape[1] // 2
     heads = width // HD
     groups = rows * cols // QUAD
-    fresh = jnp.transpose(fresh_kv, (0, 2, 1, 3))
-    prev = jnp.transpose(prev_kv, (1, 0, 2))
-    powers = jnp.transpose(exps, (1, 0, 2))
+    powers = jnp.transpose(exps, (2, 1, 0))
     q_parts = 3
     vmem = pl.BlockSpec(memory_space=pltpu.VMEM)
     anywhere = pl.BlockSpec(memory_space=pl.ANY)
@@ -332,7 +331,7 @@
         compiler_params=pltpu.CompilerParams(
             collective_id=0, has_side_effects=True, vmem_limit_bytes=60 * 2**20
         ),
-    )(hidden.reshape(STEPS * tok, depth), w_q, fresh, prev, powers, w_out)
+    )(hidden.reshape(STEPS * tok, depth), w_q, fresh_kv, prev_kv, powers, w_out)
 
 
 def solution(mesh):

time: 45.3 us -> 40.2 us (0.89)
  local copies, waits for them, and re-layouts: 6.69 us -> 1.8 us
    unnamed x4 -> x1, local copies, waits for them, and re-layouts: 6.69 us -> 1.8 us
where the time goes in v4:
time: 40.2 us; the launch traced here: 40 us
  Pallas kernels  38.2 us (95%)
  local copies, waits for them, and re-layouts  1.8 us (4%)
    pallas_call x1, Pallas kernels, on_device(): pl.pallas_call(functools.partial(kernel, rows, cols), out_shape=jax.Shape...  38.2 us
    unnamed x1, local copies, waits for them, and re-layouts  1.8 us

profile of v4, /device:TPU:1, one launch (start us, length us, event | category | flops | bytes accessed | tf_op | source)
XLA Modules:
  0.0 40.0 jit_solution(16823111528776149471)
XLA Ops:
  0.0 38.2 %shard_map.64 = bf16[2,72,1536]{2,1,0:T(8,128)(2,1)} custom-call(bf16[144,3072]{1,0:T(8,128)(2,1)} %bitcast.2, bf16[3072,768]{1,0:T(8,128)(2,1)} %w_q.1, bf16[2,72,2,768]{3,2,1,0:T(2,128)(2,1)} %fresh.1, bf16[72,2,768]{2,1,0:T(2,128)(2,1)} %prev.1, s32[6,2,72]{2,1,0:T(2,128)} %bitcast.3, bf16[768,3072]{1,0:T(8,128)(2,1)} %w_out.1), custom_call_target="tpu_custom_call" | custom-call | tf_op jit(solution)/shard_map/pallas_call | solution.py:295
  38.2 1.8 %copy.8 = bf16[2,72,1536]{2,1,0:T(8,128)(2,1)} copy(bf16[2,72,1536]{2,1,0:T(8,128)(2,1)} %shard_map.64) | data formatting | bytes 884736
